TPU v7x, 256 devices: a whole 4x4x8 slice. The times are simulated.
256 devices in a mesh: dp: 128 (over z, x, y), pair: 2 (over core).
Axes of the slice: x: 4, y: 4, z: 8, core: 2. Of those that a mesh axis runs over, the one named last changes fastest.
Arguments:
- embeddings: float32 [65536, 1024], P(('dp', 'pair')), may hold values from -140 to 140
- block_ids: int32 [128, 2, 512], replicated, may hold values from 0 to 65536, as said below
- block_counts: int32 [128], replicated, may hold values from 0 to 2, as said below
Outputs:
- max_similarity: float32 [65536], P(('dp', 'pair'))
Inputs may be any that keep to these rules, and one draw needn't show every extreme that they name: `block_ids`: every document stands in exactly one live slot of one cluster; slots past a cluster's block_counts and the tail of its last block hold 65536; each device gives exactly 4 documents to clusters 2 i and 2 i + 1 together, and at most 4 to one cluster; some cluster takes 4 documents from every device and fills its 2 blocks. `block_counts`: the number of blocks that a cluster's documents fill.
All inputs are finite; a program needn't handle non-finite values.
Results may differ from a plain program's by a relative error of at most 0.0018.
Values may be sent and summed in bfloat16 or wider, within the bound.
No kernel may reach another device: no remote copies, remote signals or barrier semaphores. Data moves between devices by JAX's collectives and lax.ppermute only.
A program may use at most 64 MiB of HBM per device.

v0:
```python
from functools import partial
import jax
import jax.numpy as jnp
from jax import lax
from jax.sharding import PartitionSpec as P


def keep_same(best_sim):
    return best_sim


def strip_scores(members, live_slots, block_rows, row_block, best_sim):
    start_row = row_block * block_rows
    rows_first = members[start_row : start_row + block_rows]
    columns = members[start_row:]
    live_first = live_slots[start_row : start_row + block_rows]
    live_columns = live_slots[start_row:]
    scores = jnp.dot(rows_first, columns.T, preferred_element_type=jnp.float32)
    same_cell = jnp.arange(block_rows)[:, None] == jnp.arange(columns.shape[0])[None, :]
    row_best = jnp.max(jnp.where(live_columns[None, :] & ~same_cell, scores, -1.0), axis=1)
    col_best = jnp.max(jnp.where(live_first[:, None] & ~same_cell, scores, -1.0), axis=0)
    best_sim = best_sim.at[start_row:].set(jnp.maximum(best_sim[start_row:], col_best))
    return best_sim.at[start_row : start_row + block_rows].set(
        jnp.maximum(best_sim[start_row : start_row + block_rows], row_best)
    )


def body(embeddings, block_ids, block_counts):
    doc_rows, feature = embeddings.shape
    chip_count = lax.axis_size("dp")
    my_chip = lax.axis_index("dp")
    my_core = lax.axis_index("pair")
    cluster_total, max_blocks, block_rows = block_ids.shape
    slot_total = max_blocks * block_rows
    doc_total = doc_rows * 2 * chip_count
    capacity = 2 * doc_rows // chip_count
    id_table = block_ids.reshape(cluster_total, slot_total)
    slot_index = jnp.arange(slot_total, dtype=jnp.int32)
    live_table = (slot_index[None, :] // block_rows < block_counts[:, None]) & (
        id_table < doc_total
    )
    square = jnp.sum(embeddings * embeddings, axis=1, keepdims=True)
    normed = (embeddings * lax.rsqrt(square + 1e-06)).astype(jnp.bfloat16)
    group_size = 1
    first_doc = (my_chip * 2 + my_core) * doc_rows
    group_span = group_size * doc_rows
    width_cap = group_size * capacity
    mine_slots = live_table & (id_table >= first_doc) & (id_table < first_doc + group_span)
    block_index = jnp.arange(block_rows, dtype=jnp.int32)
    strict_upper = (block_index[:, None] < block_index[None, :]).astype(jnp.bfloat16)
    mine_blocks = mine_slots.reshape(cluster_total * max_blocks, block_rows).astype(jnp.bfloat16)
    within_rank = jnp.dot(mine_blocks, strict_upper, preferred_element_type=jnp.float32).astype(
        jnp.int32
    )
    block_total = jnp.sum(
        mine_slots.reshape(cluster_total, max_blocks, block_rows).astype(jnp.int32), axis=2
    )
    block_before = jnp.cumsum(block_total, axis=1) - block_total
    send_rank = (
        within_rank.reshape(cluster_total, max_blocks, block_rows) + block_before[:, :, None]
    ).reshape(cluster_total, slot_total)
    rank_slot = jnp.arange(width_cap, dtype=jnp.int32)
    chosen = mine_slots[:, None, :] & (send_rank[:, None, :] == rank_slot[None, :, None])
    local_offset = (id_table - first_doc)[:, None, :]
    local_at = jnp.sum(jnp.where(chosen, local_offset, 0), axis=2) + jnp.where(
        jnp.any(chosen, axis=2), 0, group_span
    )
    doc_index = jnp.arange(group_span, dtype=jnp.int32)
    pick_docs = local_at.reshape(-1)[:, None] == doc_index[None, :]
    packed = jnp.dot(
        pick_docs.astype(jnp.bfloat16), normed, preferred_element_type=jnp.float32
    ).astype(jnp.bfloat16)
    packed = packed.reshape(cluster_total, width_cap, feature)
    received = lax.all_to_all(packed, "dp", split_axis=0, concat_axis=0, tiled=True)
    own_ids = lax.dynamic_index_in_dim(id_table, my_chip, 0, keepdims=False)
    own_live = lax.dynamic_index_in_dim(live_table, my_chip, 0, keepdims=False)
    live_blocks = lax.dynamic_index_in_dim(block_counts, my_chip, 0, keepdims=False)
    group_total = 2 * chip_count // group_size
    src_group = jnp.where(own_live, own_ids // group_span, group_total)
    earlier_same = (
        (src_group[:, None] == src_group[None, :])
        & own_live[None, :]
        & (slot_index[:, None] > slot_index[None, :])
    )
    own_rank = jnp.sum(earlier_same.astype(jnp.int32), axis=1)
    gathered = lax.all_gather(received, "pair", axis=0, tiled=True)
    row_pool = gathered.reshape(2 * chip_count * capacity, feature)
    dest_chip = src_group // 2
    source_core = src_group % 2
    pool_row = (source_core * chip_count + dest_chip) * capacity + own_rank
    accept_slot = own_live & (source_core == my_core)
    pool_row = jnp.where(own_live, pool_row, row_pool.shape[0])
    pool_index = jnp.arange(row_pool.shape[0], dtype=jnp.int32)
    pick_rows = (pool_row[:, None] == pool_index[None, :]).astype(jnp.bfloat16)
    members = jnp.dot(pick_rows, row_pool, preferred_element_type=jnp.float32).astype(jnp.bfloat16)
    best_sim = jnp.full((slot_total,), -1.0, jnp.float32)
    for row_block in range(max_blocks):
        taken = (row_block % 2 == my_core) & (row_block < live_blocks)
        best_sim = lax.cond(
            taken,
            partial(strip_scores, members, own_live, block_rows, row_block),
            keep_same,
            best_sim,
        )
    best_sim = lax.pmax(best_sim, "pair")
    target_slot = jnp.where(accept_slot, dest_chip * width_cap + own_rank, chip_count * width_cap)
    buffer_index = jnp.arange(chip_count * width_cap, dtype=jnp.int32)
    lands = target_slot[None, :] == buffer_index[:, None]
    back_buffer = jnp.max(jnp.where(lands, best_sim[None, :], -1.0), axis=1)
    returned = lax.all_to_all(
        back_buffer.reshape(chip_count, width_cap), "dp", split_axis=0, concat_axis=0, tiled=True
    )
    result = jnp.max(jnp.where(pick_docs, returned.reshape(-1)[:, None], -1.0), axis=0)
    return result


def solution(mesh):
    in_specs = (P(("dp", "pair"), None), P(), P())
    out_specs = P(("dp", "pair"))
    return jax.shard_map(body, mesh=mesh, in_specs=in_specs, out_specs=out_specs, check_vma=False)
```

profile of v0, /device:TPU:1, one launch (start us, length us, event | category | flops | bytes accessed | tf_op | source)
XLA Modules:
  0.0 124.0 jit_solution(2684171854075505043)
XLA Ops:
  6.5 0.0 all-gather.2.cloned.1.call-start
  6.6 1.4 %multiply_reduce_fusion = f32[256]{0:T(256)S(1)} fusion(f32[256,1024]{1,0:T(8,128)} %param.17), kind=kLoop, calls=%fused_computation.37 | loop fusion | flops 524032 | bytes 1049600 | tf_op jit(solution)/shard_map/reduce_sum | solution.py:42
  8.0 0.8 lt.113
  8.8 0.1 lt.114
  9.0 0.1 lt.111
  9.1 0.4 lt.112
  9.5 0.0 copy-done.1
  9.5 0.1 copy.7
  9.6 3.7 %fusion.17 = (s32[128,2]{1,0:T(8,128)S(1)}, pred[128,2,512]{2,1,0:T(4,128)(4,1)S(1)}, pred[128,2,512]{2,1,0:T(4,128)(4,1)S(1)}, pred[128,2,512]{2,1,0:T(4,128)(4,1)S(1)}) fusion(s32[2,512]{1,0:T(2,128)S(1)} %and_select_fusion.4, s32[128]{0:T(128)S(1)} %copy-done.2, s32[128,2,512]{2,1,0:T(2,128)S(1)} %copy-done.1, s32[]{:T(128)S(6)} %mul.39, s32[]{:T(128)S(6)} %add.116), kind=kLoop, calls=%fused_computation.43 | loop fusion | flops 1179392 | bytes 923144 | tf_op jit(solution)/shard_map/reduce_sum | solution.py:55
  13.4 0.3 compare_and_fusion
  13.6 0.3 lt.119
  14.0 0.2 reduce_window_sum.11
  14.2 0.3 ge.23
  14.5 0.3 lt.122
  14.8 0.4 convolution_convert_fusion.1
  15.2 0.2 reshape.352
  15.4 0.2 add.117
  15.6 0.0 copy-start
  15.6 0.1 copy.8
  15.7 0.1 add.119
  15.8 0.4 fusion.14
  16.2 0.5 select_reduce_fusion.5
  16.7 0.1 copy.5
  16.8 0.1 add.121
  16.9 0.5 convolution_convert_fusion
  17.4 0.4 reshape.353
  17.9 44.8 %all_to_all.14 = bf16[128,4,1024]{2,1,0:T(4,128)(2,1)} all-to-all(bf16[128,4,1024]{2,1,0:T(4,128)(2,1)S(1)} %reshape.353), channel_id=1, replica_groups=mesh['dp'=128,'pair'=2] {'dp'}, dimensions={0} | all-to-all | bytes 2097152 | tf_op jit(solution)/shard_map/all_to_all | solution.py:74
  62.7 0.0 all-gather.2.cloned.1.call-update
  62.8 0.6 dynamic_slice.14
  64.8 0.6 convert_reduce_fusion
  65.5 10.3 %all-gather.2.cloned.1.call-done = bf16[256,4,1024]{2,1,0:T(4,128)(2,1)} async-done(((bf16[128,4,1024]{2,1,0:T(4,128)(2,1)}), bf16[256,4,1024]{2,1,0:T(4,128)(2,1)}) %all-gather.2.cloned.1.call-update) | async-done | bytes 2097168 | tf_op jit(solution)/shard_map/all_gather | solution.py:86
  75.7 2.5 %reshape.354 = bf16[1024,1024]{1,0:T(8,128)(2,1)S(1)} reshape(bf16[256,4,1024]{2,1,0:T(4,128)(2,1)} %all-gather.2.cloned.1.call-done) | data formatting | bytes 4194304 | tf_op jit(solution)/shard_map/reshape | solution.py:87
  78.3 3.7 %fusion.15 = bf16[1024,1024]{1,0:T(8,128)(2,1)} fusion(bf16[1024,1024]{1,0:T(8,128)(2,1)S(1)} %reshape.354, s32[1024]{0:T(1024)S(1)} %fusion.30), kind=kOutput, calls=%fused_computation.33 | convolution fusion | flops 2149580800 | bytes 4198400 | tf_op jit(solution)/shard_map/dot_general | solution.py:95
  82.0 0.6 conditional.2
  82.0 0.6 broadcast_in_dim.55
  82.6 4.6 %conditional.3 = (f32[1024]{0:T(1024)}) conditional(s32[]{:T(128)} %convert_element_type.31, f32[1024]{0:T(1024)} %get-tuple-element.95, (f32[1024]{0:T(1024)}, pred[1024]{0:T(1024)(128)(4,1)S(1)}, bf16[1024,1024]{1,0:T(8,128)(2,1)}) %tuple.38), branch_computations={%region_10.11_spmd, %region_11.14_spmd} | conditional | flops 538968576 | bytes 1085448 | solution.py:99
  82.6 2.5 %select_reduce_fusion.2 = (f32[512]{0:T(512)S(1)}, f32[512]{0:T(512)S(1)}) fusion(pred[512]{0:T(512)(128)(4,1)S(1)} %slice.66, bf16[1024,1024]{1,0:T(8,128)(2,1)} %get-tuple-element.82), kind=kOutput, calls=%fused_computation.10 | convolution fusion | flops 538967040 | bytes 1053696 | tf_op jit(solution)/shard_map/cond/branch_1_fun/dot_general | solution.py:18
  85.2 0.7 copy.9
  85.9 0.7 maximum_dynamic-update-slice_fusion.1
  86.6 0.6 copy.15
  87.2 3.3 %pmax.7 = f32[1024]{0:T(1024)S(1)} all-reduce(f32[1024]{0:T(1024)} %get-tuple-element.96), channel_id=1, replica_groups=mesh['dp'=128,'pair'=2] {'pair'}, use_global_device_ids=true, to_apply=%region_14.15 | all-reduce | flops 1024 | bytes 8192 | tf_op jit(solution)/shard_map/pmax | solution.py:105
  90.4 0.3 select_reduce_fusion.4
  90.7 0.1 all_to_all.10
  90.8 24.1 %all_to_all.15 = f32[128,1,4]{2,1,0:T(1,128)S(1)} all-to-all(f32[128,1,4]{2,1,0:T(1,128)S(1)} %bitcast.21), channel_id=1, replica_groups=mesh['dp'=128,'pair'=2] {'dp'}, dimensions={0} | all-to-all | bytes 4096 | tf_op jit(solution)/shard_map/all_to_all | solution.py:110
  114.9 0.5 broadcast.371
  115.4 0.8 reduce.13
  116.3 0.1 broadcast_in_dim.106
  116.4 0.8 select_reduce_fusion.6
  (17 shorter events, 0.3 us)
Async XLA Ops:
  6.5 2.9 %copy-start.1 = (s32[128,2,512]{2,1,0:T(2,128)S(1)}, s32[128,2,512]{2,1,0:T(2,128)}, u32[]{:S(2)}) copy-start(s32[128,2,512]{2,1,0:T(2,128)} %param.18) | copy-start | bytes 1572868
  6.5 69.2 %all-gather.2.cloned.1.call-start = ((), (), s32[]{:S(2)}) async-start(), calls=%async_computation.2 | async-start | bytes 3145728 | tf_op jit(solution)/shard_map/all_gather | solution.py:86
  8.0 1.6 %copy-start.2 = (s32[128]{0:T(128)S(1)}, s32[128]{0:T(128)}, u32[]{:S(2)}) copy-start(s32[128]{0:T(128)} %param.19) | copy-start | bytes 1540
  15.6 1.3 %copy-start = (f32[256,1024]{1,0:T(8,128)S(1)}, f32[256,1024]{1,0:T(8,128)}, u32[]{:S(2)}) copy-start(f32[256,1024]{1,0:T(8,128)} %param.17) | copy-start | bytes 3145732
Sparse Core Ops, SparseCore 0:
  62.9 12.8 all-gather.1
where the time goes:
time: 124 us
  blocking collectives  72.2 us (58%)
  between operations  15 us (12%)
  waiting for transfers between devices  10.3 us (8%)
  other arithmetic  9.97 us (8%)
  local copies, waits for them, and re-layouts  9.37 us (8%)
  matrix products  7.18 us (6%)
    all_to_all x1, blocking collectives, body(): lax.all_to_all(packed, 'dp', split_axis=0, concat_axis=0, tiled=True)  44.8 us
    all_to_all x1, blocking collectives, body(): lax.all_to_all(back_buffer.reshape(chip_count, width_cap), 'dp', split_ax...  24.1 us
    all_gather x1, waiting for transfers between devices, body(): gathered = lax.all_gather(received, 'pair', axis=0, tiled=True)  10.3 us
    reduce_sum x1, other arithmetic, body(): jnp.sum(mine_slots.reshape(cluster_total, max_blocks, block_rows).astype(...  3.73 us
    dot_general x1, matrix products, body(): jnp.dot(pick_rows, row_pool, preferred_element_type=jnp.float32)  3.73 us
    pmax x1, blocking collectives, body(): best_sim = lax.pmax(best_sim, 'pair')  3.25 us
    dot_general x1, matrix products, strip_scores(): scores = jnp.dot(rows_first, columns.T, preferred_element_type=jnp.float32)  2.54 us
    reshape x1, local copies, waits for them, and re-layouts, body(): row_pool = gathered.reshape(2 * chip_count * capacity, feature)  2.54 us
  transfers between devices with their start and end apart: 1, of which 1 were waited for; matrix products, arithmetic and copies ran while one was open for 1% of the time, Pallas kernels for 0%

commit v1 on v0

--- a/solution.py
+++ b/solution.py
@@ -3,6 +3,13 @@
 import jax.numpy as jnp
 from jax import lax
 from jax.sharding import PartitionSpec as P
+
+
+def exchange_gather(value, name, along):
+    size = lax.axis_size(name)
+    blocks = jnp.stack([value for _ in range(size)])
+    blocks = lax.all_to_all(blocks, name, split_axis=0, concat_axis=0)
+    return jnp.concatenate(blocks, axis=along)
 
 
 def keep_same(best_sim):
@@ -83,7 +90,7 @@
         & (slot_index[:, None] > slot_index[None, :])
     )
     own_rank = jnp.sum(earlier_same.astype(jnp.int32), axis=1)
-    gathered = lax.all_gather(received, "pair", axis=0, tiled=True)
+    gathered = exchange_gather(received, "pair", 0)
     row_pool = gathered.reshape(2 * chip_count * capacity, feature)
     dest_chip = src_group // 2
     source_core = src_group % 2

time: 124 us -> 98.8 us (0.80)
  blocking collectives: 72.2 us -> 28.1 us
  starting transfers between devices: 0.01 us -> 16.3 us
  waiting for transfers between devices: 10.3 us -> 25.9 us
  between operations: 15 us -> 1.57 us
  matrix products: 7.18 us -> 5.75 us
    all_to_all x1, blocking collectives: 44.8 us -> 8.63 us  [exchange_gather(): blocks = lax.all_to_all(blocks, name, split_axis=0, concat_axis=0)]
    all_to_all x0 -> x1, waiting for transfers between devices: none -> 25.9 us  [body(): lax.all_to_all(packed, 'dp', split_axis=0, concat_axis=0, tiled=True)]
    all_to_all x0 -> x1, starting transfers between devices: none -> 16.3 us  [body(): lax.all_to_all(packed, 'dp', split_axis=0, concat_axis=0, tiled=True)]
    all_gather x1 -> x0, waiting for transfers between devices: 10.3 us -> none  [body(): gathered = lax.all_gather(received, 'pair', axis=0, tiled=True)]
    all_to_all x1, blocking collectives: 24.1 us -> 16.4 us  [body(): lax.all_to_all(back_buffer.reshape(chip_count, width_cap), 'dp', split_ax...]
    reshape x1 -> x0, local copies, waits for them, and re-layouts: 2.54 us -> none  [body(): row_pool = gathered.reshape(2 * chip_count * capacity, feature)]
    another operation x0 -> x1, local copies, waits for them, and re-layouts: none -> 2.07 us  [body(): row_pool = gathered.reshape(2 * chip_count * capacity, feature)]
    dot_general x1, matrix products: 2.54 us -> 0.88 us  [strip_scores(): scores = jnp.dot(rows_first, columns.T, preferred_element_type=jnp.float32)]
where the time goes in v1:
time: 98.8 us; the launch traced here: 98.3 us
  blocking collectives  28.1 us (28%)
  waiting for transfers between devices  25.9 us (26%)
  starting transfers between devices  16.3 us (16%)
  other arithmetic  10.9 us (11%)
  local copies, waits for them, and re-layouts  9.7 us (10%)
  matrix products  5.75 us (6%)
  between operations  1.57 us (2%)
    all_to_all x1, waiting for transfers between devices, body(): lax.all_to_all(packed, 'dp', split_axis=0, concat_axis=0, tiled=True)  25.9 us
    all_to_all x1, blocking collectives, body(): lax.all_to_all(back_buffer.reshape(chip_count, width_cap), 'dp', split_ax...  16.4 us
    all_to_all x1, starting transfers between devices, body(): lax.all_to_all(packed, 'dp', split_axis=0, concat_axis=0, tiled=True)  16.3 us
    all_to_all x1, blocking collectives, exchange_gather(): blocks = lax.all_to_all(blocks, name, split_axis=0, concat_axis=0)  8.63 us
    dot_general x1, matrix products, body(): jnp.dot(pick_rows, row_pool, preferred_element_type=jnp.float32)  3.96 us
    reduce_sum x1, other arithmetic, body(): jnp.sum(mine_slots.reshape(cluster_total, max_blocks, block_rows).astype(...  3.73 us
    pmax x1, blocking collectives, body(): best_sim = lax.pmax(best_sim, 'pair')  3.12 us
    another operation x1, local copies, waits for them, and re-layouts, body(): row_pool = gathered.reshape(2 * chip_count * capacity, feature)  2.07 us
  transfers between devices with their start and end apart: 1, of which 1 were waited for; matrix products, arithmetic and copies ran while one was open for 1% of the time, Pallas kernels for 0%

profile of v1, /device:TPU:1, one launch (start us, length us, event | category | flops | bytes accessed | tf_op | source)
XLA Modules:
  0.0 98.3 jit_solution(1701770429457501776)
XLA Ops:
  0.0 1.4 %multiply_reduce_fusion = f32[256]{0:T(256)S(1)} fusion(f32[256,1024]{1,0:T(8,128)} %param.17), kind=kLoop, calls=%fused_computation.38 | loop fusion | flops 524032 | bytes 1049600 | tf_op jit(solution)/shard_map/reduce_sum | solution.py:49
  1.5 0.8 lt.113
  2.3 0.1 lt.114
  2.4 0.1 lt.111
  2.6 0.4 lt.112
  2.9 0.0 copy-done.1
  2.9 0.1 copy.7
  3.1 3.7 %fusion.17 = (s32[128,2]{1,0:T(8,128)S(1)}, pred[128,2,512]{2,1,0:T(4,128)(4,1)S(1)}, pred[128,2,512]{2,1,0:T(4,128)(4,1)S(1)}, pred[128,2,512]{2,1,0:T(4,128)(4,1)S(1)}) fusion(s32[2,512]{1,0:T(2,128)S(1)} %and_select_fusion.4, s32[128]{0:T(128)S(1)} %copy-done.2, s32[128,2,512]{2,1,0:T(2,128)S(1)} %copy-done.1, s32[]{:T(128)S(6)} %mul.39, s32[]{:T(128)S(6)} %add.116), kind=kLoop, calls=%fused_computation.44 | loop fusion | flops 1179392 | bytes 923144 | tf_op jit(solution)/shard_map/reduce_sum | solution.py:62
  6.8 0.3 compare_and_fusion
  7.1 0.3 lt.119
  7.4 0.2 reduce_window_sum.11
  7.6 0.3 ge.23
  7.9 0.3 lt.122
  8.3 0.4 convolution_convert_fusion.1
  8.7 0.2 reshape.349
  8.8 0.2 add.117
  9.0 0.0 copy-start
  9.1 0.1 copy.8
  9.2 0.1 add.119
  9.2 0.4 fusion.14
  9.6 0.5 select_reduce_fusion.5
  10.2 0.1 copy.5
  10.3 0.1 add.121
  10.4 0.5 convolution_convert_fusion
  10.9 1.2 %reshape.350 = bf16[128,4,1024]{2,1,0:T(4,128)(2,1)} reshape(bf16[512,1024]{1,0:T(8,128)(2,1)S(1)} %convolution_convert_fusion) | data formatting | bytes 2097152 | tf_op jit(solution)/shard_map/reshape | solution.py:80
  12.1 16.3 %all-to-all-start = ((bf16[128,4,1024]{2,1,0:T(4,128)(2,1)}), bf16[128,4,1024]{2,1,0:T(4,128)(2,1)S(1)}, u32[]{:S(2)}, u32[]{:S(2)}) async-start(bf16[128,4,1024]{2,1,0:T(4,128)(2,1)} %reshape.350), calls=%async_computation | async-start | bytes 2097152 | tf_op jit(solution)/shard_map/all_to_all | solution.py:81
  28.5 0.6 dynamic_slice.14
  30.5 0.6 convert_reduce_fusion
  31.2 25.9 %all-to-all-done = bf16[128,4,1024]{2,1,0:T(4,128)(2,1)S(1)} async-done(((bf16[128,4,1024]{2,1,0:T(4,128)(2,1)}), bf16[128,4,1024]{2,1,0:T(4,128)(2,1)S(1)}, u32[]{:S(2)}, u32[]{:S(2)}) %all-to-all-start) | async-done | bytes 1048608 | tf_op jit(solution)/shard_map/all_to_all | solution.py:81
  57.1 1.0 pad_maximum_fusion
  58.0 8.6 %all_to_all.19 = bf16[2,128,4,1024]{3,2,1,0:T(4,128)(2,1)S(1)} all-to-all(bf16[2,128,4,1024]{3,2,1,0:T(4,128)(2,1)S(1)} %pad_maximum_fusion), channel_id=1, replica_groups=mesh['dp'=128,'pair'=2] {'pair'}, dimensions={0} | all-to-all | bytes 4194304 | tf_op jit(solution)/shard_map/all_to_all | solution.py:11
  66.7 2.1 %reshape_reshape.3 = bf16[1024,1024]{1,0:T(8,128)(2,1)} reshape(bf16[2,128,4,1024]{3,2,1,0:T(4,128)(2,1)S(1)} %all_to_all.19) | data formatting | bytes 4194304 | tf_op jit(solution)/shard_map/reshape;reshape | solution.py:94
  68.7 4.0 %fusion.15 = bf16[1024,1024]{1,0:T(8,128)(2,1)S(1)} fusion(bf16[1024,1024]{1,0:T(8,128)(2,1)} %reshape_reshape.3, s32[1024]{0:T(1024)S(1)} %fusion.30), kind=kOutput, calls=%fused_computation.34 | convolution fusion | flops 2149580800 | bytes 4198400 | tf_op jit(solution)/shard_map/dot_general | solution.py:102
  72.7 0.6 conditional.2
  72.7 0.6 broadcast_in_dim.55
  73.3 2.9 %conditional.3 = (f32[1024]{0:T(1024)}) conditional(s32[]{:T(128)} %convert_element_type.31, f32[1024]{0:T(1024)} %get-tuple-element.95, (f32[1024]{0:T(1024)}, pred[1024]{0:T(1024)(128)(4,1)S(1)}, bf16[1024,1024]{1,0:T(8,128)(2,1)S(1)}) %tuple.38), branch_computations={%region_10.11_spmd, %region_11.14_spmd} | conditional | flops 538968576 | bytes 1085448 | solution.py:106
  73.3 0.9 select_reduce_fusion.2
  74.2 0.7 copy.9
  74.9 0.7 maximum_dynamic-update-slice_fusion.1
  75.6 0.6 copy.15
  76.2 3.1 %pmax.7 = f32[1024]{0:T(1024)S(1)} all-reduce(f32[1024]{0:T(1024)} %get-tuple-element.96), channel_id=1, replica_groups=mesh['dp'=128,'pair'=2] {'pair'}, use_global_device_ids=true, to_apply=%region_14.15 | all-reduce | flops 1024 | bytes 8192 | tf_op jit(solution)/shard_map/pmax | solution.py:112
  79.3 0.3 select_reduce_fusion.4
  79.6 0.1 all_to_all.14
  79.7 16.4 %all_to_all.20 = f32[128,1,4]{2,1,0:T(1,128)S(1)} all-to-all(f32[128,1,4]{2,1,0:T(1,128)S(1)} %bitcast.23), channel_id=1, replica_groups=mesh['dp'=128,'pair'=2] {'dp'}, dimensions={0} | all-to-all | bytes 4096 | tf_op jit(solution)/shard_map/all_to_all | solution.py:117
  96.1 0.5 broadcast.371
  96.6 0.8 reduce.13
  97.5 0.1 broadcast_in_dim.106
  97.6 0.8 select_reduce_fusion.6
  (17 shorter events, 0.3 us)
Async XLA Ops:
  0.0 2.9 %copy-start.1 = (s32[128,2,512]{2,1,0:T(2,128)S(1)}, s32[128,2,512]{2,1,0:T(2,128)}, u32[]{:S(2)}) copy-start(s32[128,2,512]{2,1,0:T(2,128)} %param.18) | copy-start | bytes 1572868
  1.5 1.6 %copy-start.2 = (s32[128]{0:T(128)S(1)}, s32[128]{0:T(128)}, u32[]{:S(2)}) copy-start(s32[128]{0:T(128)} %param.19) | copy-start | bytes 1540
  9.0 1.3 %copy-start = (f32[256,1024]{1,0:T(8,128)S(1)}, f32[256,1024]{1,0:T(8,128)}, u32[]{:S(2)}) copy-start(f32[256,1024]{1,0:T(8,128)} %param.17) | copy-start | bytes 3145732
  12.1 44.9 %all-to-all-start = ((bf16[128,4,1024]{2,1,0:T(4,128)(2,1)}), bf16[128,4,1024]{2,1,0:T(4,128)(2,1)S(1)}, u32[]{:S(2)}, u32[]{:S(2)}) async-start(bf16[128,4,1024]{2,1,0:T(4,128)(2,1)} %reshape.350), calls=%async_computation | async-start | bytes 2097152 | tf_op jit(solution)/shard_map/all_to_all | solution.py:81
